TPU v7x, 256 devices: a whole 4x4x8 slice. The times are simulated.
256 devices in a mesh: walk: 64 (over x, z, core), vec: 4 (over y).
Axes of the slice: x: 4, y: 4, z: 8, core: 2. Of those that a mesh axis runs over, the one named last changes fastest.
Arguments:
- walkers: bfloat16 [128, 2432, 768], P('walk')
- chol: bfloat16 [4, 64, 384, 4096], P('vec', 'walk'), may hold values from -6 to 6
- owners: int32 [4, 2], P('vec'), may hold values from 0 to 63
- branch_src: int32 [128], P('walk'), may hold values from 0 to 127, as said below
Outputs:
- branched: bfloat16 [128, 2432, 768], P('walk')
- force_bias: float32 [128, 8, 2], P('walk', 'vec')
- exchange: float32 [128, 2], P('walk')
Inputs may be any that keep to these rules, and one draw needn't show every extreme that they name: `branch_src`: slot s takes its walker from the 2 walkers of block s // 2, or of the block before or after it (blocks taken cyclically).
All inputs are finite; a program needn't handle non-finite values.
Results may differ from a plain program's by a relative error of at most 0.0052.
Values may be sent and summed in bfloat16 or wider, within the bound.
No kernel may reach another device: no remote copies, remote signals or barrier semaphores. Data moves between devices by JAX's collectives and lax.ppermute only.
A program may use at most 192 MiB of HBM per device.

v0:
```python
import jax
import jax.numpy as jnp
from jax import lax
from jax.experimental import pallas as pl
from jax.experimental.pallas import tpu as pltpu
from jax.sharding import PartitionSpec as P

NX, NZ, NC, NY = 4, 8, 2, 4


def walk_index(x, z, c):
    return ((x % NX) * NZ + z % NZ) * NC + c % NC


def chips():
    return [(x, z, c) for x in range(NX) for z in range(NZ) for c in range(NC)]


def to_chip(dx, dz):
    return [(walk_index(x, z, c), walk_index(x + (1 - 2 * c) * dx, z + (1 - 2 * c) * dz, c)) for x, z, c in chips()]


def ring(size, step):
    return [(i, (i + step) % size) for i in range(size)]


def across_chips():
    size = NX * NZ * NC
    return [(i, (i + 1) % size if i % NC == 1 else (i - 1) % size) for i in range(size)]


def terms_kernel(place_ref, *refs):
    pieces, (w_ref, out_ref, acc_ref, m_ref) = refs[:2 * NX], refs[2 * NX:]
    half, depth = pieces[0].shape
    electrons, orbitals = NC * half, 2 * depth
    for side in range(NC):
        acc_ref[...] = jnp.zeros_like(acc_ref)
        for k in range(NX):
            block = place_ref[side * NX + k]
            rows = pl.ds(pl.multiple_of(lax.rem(block, 2) * depth, depth), depth)
            acc_ref[lax.div(block, 2)] += jnp.dot(
                pieces[side * NX + k][...], w_ref[0, rows, :], preferred_element_type=jnp.float32
            )
        by_real, by_imag = acc_ref[0], acc_ref[1]
        place = pl.ds(pl.multiple_of(place_ref[NC * NX + side] * half, half), half)
        m_ref[0, place, :] = (by_real[:, :electrons] - by_imag[:, electrons:]).astype(jnp.bfloat16)
        m_ref[1, place, :] = (by_real[:, electrons:] + by_imag[:, :electrons]).astype(jnp.bfloat16)
    inverse = w_ref[0, orbitals:, :]
    g_by_real = jnp.dot(m_ref[0], inverse, preferred_element_type=jnp.float32)
    g_by_imag = jnp.dot(m_ref[1], inverse, preferred_element_type=jnp.float32)
    real = g_by_real[:, :electrons] - g_by_imag[:, electrons:]
    imag = g_by_real[:, electrons:] + g_by_imag[:, :electrons]
    real_t = real.T
    rows = lax.broadcasted_iota(jnp.int32, real.shape, 0)
    columns = lax.broadcasted_iota(jnp.int32, real.shape, 1)
    diagonal = rows == columns
    values = (
        jnp.sum(jnp.where(diagonal, real, 0.0)),
        jnp.sum(jnp.where(diagonal, imag, 0.0)),
        jnp.sum(real * real_t - imag * imag.T),
        2.0 * jnp.sum(imag * real_t),
    )
    lane = lax.broadcasted_iota(jnp.int32, out_ref.shape, 2)
    row = jnp.zeros(out_ref.shape, jnp.float32)
    for place, value in enumerate(values):
        row = jnp.where(lane == place, value, row)
    out_ref[...] = row


def walker_terms(place, pieces, walkers):
    count, height, width = walkers.shape
    half, depth = pieces[0].shape
    electrons = NC * half
    whole = pl.BlockSpec((half, depth), lambda i, _: (0, 0))
    out = pl.pallas_call(
        terms_kernel,
        grid_spec=pltpu.PrefetchScalarGridSpec(
            num_scalar_prefetch=1,
            grid=(count,),
            in_specs=[whole] * len(pieces) + [pl.BlockSpec((1, height, width), lambda i, _: (i, 0, 0))],
            out_specs=pl.BlockSpec((1, 8, 128), lambda i, _: (i, 0, 0)),
            scratch_shapes=[
                pltpu.VMEM((2, half, width), jnp.float32),
                pltpu.VMEM((2, electrons, width // 2), jnp.bfloat16),
            ],
        ),
        out_shape=jax.ShapeDtypeStruct((count, 8, 128), jnp.float32),
        compiler_params=pltpu.CompilerParams(vmem_limit_bytes=40 * 2**20),
        cost_estimate=pl.CostEstimate(
            flops=2 * count * electrons * (2 * NX * depth // 2 + width) * width,
            bytes_accessed=2 * (len(pieces) * pieces[0].size + walkers.size),
            transcendentals=0,
        ),
    )(place, *pieces, walkers)
    return out[:, 0, :4]


def branch_kernel(plan_ref, own_ref, core_ref, q0_ref, q1_ref, q2_ref, q3_ref, out_ref, held, in_sems, out_sems):
    slots, height, _ = out_ref.shape
    part = height // NY
    quarters = (q0_ref, q1_ref, q2_ref, q3_ref)

    def rows(k):
        return pl.ds(pl.multiple_of(plan_ref[2 * slots + k] * part, 16), part)

    def fetch(slot, k, source, index):
        src = (own_ref.at[index, rows(k)], core_ref.at[index, rows(k)], quarters[k].at[index])[source]
        return pltpu.make_async_copy(src, held.at[slot, k], in_sems.at[slot, k])

    def store(slot, k):
        return pltpu.make_async_copy(held.at[slot, k], out_ref.at[slot, rows(k)], out_sems.at[slot, k])

    for slot in range(slots):
        index = plan_ref[slots + slot]
        for source in range(3):
            @pl.when(plan_ref[slot] == source)
            def _(slot=slot, index=index, source=source):
                for k in range(NY):
                    fetch(slot, k, source, index).start()
    for slot in range(slots):
        for k in range(NY):
            fetch(slot, k, 0, 0).wait()
            store(slot, k).start()
    for slot in range(slots):
        for k in range(NY):
            store(slot, k).wait()


def branch(plan, own, other_core, quarters):
    anywhere = pl.BlockSpec(memory_space=pl.ANY)
    slots, height, width = own.shape
    return pl.pallas_call(
        branch_kernel,
        in_specs=[pl.BlockSpec(memory_space=pltpu.SMEM)] + [anywhere] * 6,
        out_specs=anywhere,
        out_shape=jax.ShapeDtypeStruct(own.shape, own.dtype),
        scratch_shapes=[
            pltpu.VMEM((slots, NY, height // NY, width), own.dtype),
            pltpu.SemaphoreType.DMA((slots, NY)),
            pltpu.SemaphoreType.DMA((slots, NY)),
        ],
        compiler_params=pltpu.CompilerParams(vmem_limit_bytes=16 * 2**20),
        cost_estimate=pl.CostEstimate(flops=0, bytes_accessed=4 * own.size, transcendentals=0),
    )(plan, own, other_core, *quarters)


def after(values, *done):
    return jax.tree.unflatten(
        jax.tree.structure(values), lax.optimization_barrier((*jax.tree.leaves(values), *done))[: len(jax.tree.leaves(values))]
    )


def cut_blocks(own, swapped, owner, x, c):
    electrons, columns = own.shape
    half, depth = electrons // NC, columns // NX

    def block(place):
        cut = [lax.dynamic_slice(a, (c * half, place * depth), (half, depth)) for a in (own, swapped)]
        return jnp.where(owner % NC == c, cut[0], cut[1])

    return [block((x + (1 - 2 * c) * dx + NX * NX) % NX) for dx in (0, 1, 3, 2)]


def scatter(blocks):
    return [lax.ppermute(sent, "walk", to_chip(dx, 0)) for dx, sent in zip((1, 3, 2), blocks[1:])]


def scattered(own, arrived, owner_x, x, c):
    for dx, block in zip((1, 3, 2), arrived):
        own = jnp.where((owner_x + (1 - 2 * c) * dx + NX * NX) % NX == x, block, own)
    return own


def flood_step(up, down):
    up, down = after((up, down))
    return lax.ppermute(up, "walk", to_chip(0, 1)), lax.ppermute(down, "walk", to_chip(0, -1))


def flooded(halves, streams, away):
    first, second = halves
    for step, (up, down) in enumerate(streams, 1):
        first = jnp.where(away == step, up, first)
        second = jnp.where(away == NZ - step, down, second)
        if step > 1:
            first = jnp.where(away == NZ - (step - 1), down, first)
            second = jnp.where(away == step - 1, up, second)
    return jnp.concatenate([first, second], axis=0)


def along_x(piece):
    return [lax.ppermute(piece, "walk", to_chip(dx, 0)) for dx in (1, 3, 2)]


def to_other_core(array):
    return lax.ppermute(array, "walk", [(i, i ^ 1) for i in range(NX * NZ * NC)])


def shards(walkers, chol, owners, branch_src):
    slots, height, _ = walkers.shape
    device, y = lax.axis_index("walk"), lax.axis_index("vec")
    x, z, c = device // (NZ * NC), device // NC % NZ, device % NC
    size = NX * NZ * NC
    total = slots * size
    own = chol[0, 0]
    owner = owners[0]
    both_ways = [
        (w * NY + v, w * NY + (v + (1 if w % NC == 0 else -1)) % NY) for w in range(size) for v in range(NY)
    ]

    def pass_on(quarter):
        return lax.ppermute(quarter, ("walk", "vec"), both_ways)

    with jax.named_scope("core_swap"):
        swapped = to_other_core(own)
    with jax.named_scope("halo_z"):
        part = height // NY
        quarter = lax.dynamic_slice_in_dim(walkers, y * part, part, 1)
        owner_x = [owner[g] // (NZ * NC) for g in range(2)]
        owner_z = [owner[g] // NC % NZ for g in range(2)]
        swapped, quarter, owner_x, owner_z = after((swapped, quarter, owner_x, owner_z))
        quarters = [lax.ppermute(quarter, "walk", across_chips())]
    with jax.named_scope("core_walkers"):
        other_core = to_other_core(after(walkers, swapped))
    with jax.named_scope("blocks"):
        blocks = [cut_blocks(own, swapped, owner[g], x, c) for g in range(2)]
    half = own.shape[0] // (2 * NC)
    is_owner = [owner_z[g] == z for g in range(2)]
    away = [((1 - 2 * c) * (z - owner_z[g]) + NZ) % NZ for g in range(2)]

    def turned(g, arrived):
        return [jnp.where(is_owner[g], halves[g][1 - i], arrived[i]) for i in range(2)]

    with jax.named_scope("x_scatter_0"):
        arrived = scatter(blocks[0])
        arrived, sent, quarters[0] = after((arrived, blocks[1], quarters[0]))
        piece = scattered(blocks[0][0], arrived, owner_x[0], x, c)
        halves = [(piece[:half], piece[half:])]
        halves[0], sent, quarters[0], other_core = after((halves[0], sent, quarters[0], other_core))
    with jax.named_scope("x_scatter_1"):
        arrived = scatter(sent)
    with jax.named_scope("z_flood"):
        first = flood_step(*halves[0])
    with jax.named_scope("halo_y"):
        quarters.append(pass_on(quarters[0]))
    with jax.named_scope("x_scatter_1"):
        arrived, first, quarters[1] = after((arrived, first, quarters[1]))
        piece = scattered(sent[0], arrived, owner_x[1], x, c)
        halves.append((piece[:half], piece[half:]))
    with jax.named_scope("z_flood"):
        ahead = turned(0, first)
        second = flood_step(*[jnp.stack([ahead[i], halves[1][i]]) for i in range(2)])
        late = is_owner[1] & (jnp.arange(2) == 1)[:, None, None]
        third = flood_step(*[jnp.where(late, halves[1][1 - i][None], second[i]) for i in range(2)])
    with jax.named_scope("halo_y"):
        quarters.append(pass_on(quarters[1]))
    with jax.named_scope("z_flood"):
        third, quarters[2] = after((third, quarters[2]))
        fourth = flood_step(*third)
    with jax.named_scope("halo_y"):
        quarters.append(pass_on(quarters[2]))
    with jax.named_scope("z_flood"):
        piece = flooded(halves[0], [first] + [[a[0] for a in b] for b in (second, third, fourth)], away[0])
        fifth = flood_step(*after([a[1] for a in fourth], piece))
    with jax.named_scope("x_gather_0"):
        mine = [piece] + along_x(piece)
    with jax.named_scope("z_flood"):
        piece = flooded(halves[1], [[a[1] for a in b] for b in (second, third, fourth)] + [fifth], away[1])
        piece, mine, quarters[3] = after((piece, mine, quarters[3]))
    with jax.named_scope("core_gather_0"):
        pieces = mine + [to_other_core(p) for p in mine]
        piece, pieces = after((piece, pieces))
    relative = (branch_src - (device - 1) * slots + total) % total
    side, index = relative // slots, relative % slots
    source = jnp.where(side == 1, 0, jnp.where((side == 0) == (c == 0), 2, 1))
    held = (y + jnp.arange(NY) * jnp.where(c == 0, NY - 1, 1)) % NY
    plan = after(jnp.concatenate([source, index, held]).astype(jnp.int32), pieces[-1])
    sign = 1 - 2 * c
    columns = [(x + k + NX) % NX for k in (0, -sign, sign, 2, 0, sign, -sign, 2)]
    place = jnp.stack([*columns, c, 1 - c]).astype(jnp.int32)
    with jax.named_scope("terms_0"):
        terms = [walker_terms(place, pieces, walkers)]
    with jax.named_scope("x_gather_1"):
        ahead = lax.ppermute(piece, "walk", to_chip(1, 0))
        later, ahead = after((piece, ahead), terms[0])
        mine = [piece, ahead, *[lax.ppermute(later, "walk", to_chip(dx, 0)) for dx in (3, 2)]]
    with jax.named_scope("branch"):
        branched = branch(plan, walkers, other_core, quarters)
    with jax.named_scope("core_gather_1"):
        mine[2] = after(mine[2], branched)
        pieces = mine + [to_other_core(p) for p in mine]
    with jax.named_scope("terms_1"):
        terms.append(walker_terms(place, pieces, walkers))
    with jax.named_scope("results"):
        bias = jnp.stack([t[:, :2] for t in terms], axis=1).reshape(slots, -1)
        energy = sum(t[:, 2:] for t in terms)
        others = [lax.ppermute(energy, "vec", ring(NY, k)) for k in range(1, NY)]
        energy = (energy + others[1]) + (others[0] + others[2])
        row = jnp.concatenate([bias, -0.5 * energy], axis=1)
        left = lax.ppermute(row, "walk", ring(size, 1))
        right = lax.ppermute(row, "walk", ring(size, -1))
        rows = jnp.concatenate([left, row, right], axis=0)
        chosen = jnp.sum(jnp.where((relative[:, None] == jnp.arange(3 * slots))[:, :, None], rows[None], 0.0), axis=1)
        force_bias = chosen[:, :-2].reshape(slots, len(terms), 2)
    return branched, force_bias, chosen[:, -2:]


def solution(mesh):
    return jax.shard_map(
        shards,
        mesh=mesh,
        in_specs=(P("walk", None, None), P("vec", "walk", None, None), P("vec", None), P("walk")),
        out_specs=(P("walk", None, None), P("walk", "vec", None), P("walk", None)),
        check_vma=False,
    )
```

profile of v0, /device:TPU:24, one launch (start us, length us, event | category | flops | bytes accessed | tf_op | source)
XLA Modules:
  0.0 226.1 jit_solution(7900063300936968831)
XLA Ops:
  12.4 7.7 %collective-permute-start.4 = (bf16[2,608,768]{2,1,0:T(8,128)(2,1)}, bf16[2,608,768]{2,1,0:T(8,128)(2,1)S(1)}, u32[]{:S(2)}, u32[]{:S(2)}) collective-permute-start(bf16[2,608,768]{2,1,0:T(8,128)(2,1)} %constant_dynamic-slice_fusion), channel_id=1, source_target_pairs={{0,252},{4,8},{8,4},{12,16},{16,12},{20,24},{24,20},{28,32},{32,28... | collective-permute-start | bytes 5603336 | tf_op jit(solution)/shard_map/halo_z/ppermute | solution.py:221
  20.1 3.6 %bitcast_select_fusion.2 = (bf16[192,1024]{1,0:T(8,128)(2,1)S(1)}, bf16[192,1024]{1,0:T(8,128)(2,1)}, bf16[192,1024]{1,0:T(8,128)(2,1)}, bf16[192,1024]{1,0:T(8,...) fusion(pred[]{:T(512)S(6)} %eq.185, ...), kind=kLoop, calls=%fused_computation.9 | loop fusion | flops 1376256 | bytes 5898262 | tf_op jit(solution)/shard_map/blocks/jit(_where)/select_n | solution.py:159
  26.6 23.8 %collective-permute-done.3 = bf16[192,1024]{1,0:T(8,128)(2,1)S(1)} collective-permute-done((bf16[192,1024]{1,0:T(8,128)(2,1)}, bf16[192,1024]{1,0:T(8,128)(2,1)S(1)}, u32[]{:S(2)}, u32[]{:S(2)}) %collective-permute-start.3) | collective-permute-done | bytes 393248 | tf_op jit(solution)/shard_map/x_scatter_0/ppermute | solution.py:165
  50.4 8.2 %collective-permute-done.1 = bf16[192,1024]{1,0:T(8,128)(2,1)} collective-permute-done((bf16[192,1024]{1,0:T(8,128)(2,1)S(1)}, bf16[192,1024]{1,0:T(8,128)(2,1)}, u32[]{:S(2)}, u32[]{:S(2)}) %collective-permute-start.1) | collective-permute-done | bytes 393248 | tf_op jit(solution)/shard_map/x_scatter_0/ppermute | solution.py:165
  60.4 3.2 %collective-permute-start.7 = (bf16[192,1024]{1,0:T(8,128)(2,1)}, bf16[192,1024]{1,0:T(8,128)(2,1)}, u32[]{:S(2)}, u32[]{:S(2)}) collective-permute-start(bf16[192,1024]{1,0:T(8,128)(2,1)} %get-tuple-element.81), channel_id=1, source_target_pairs={{0,192},{4,68},{8,200},{12,76},{16,208},{20,84},{24,216},{28,92},{... | collective-permute-start | bytes 1179656 | tf_op jit(solution)/shard_map/x_scatter_1/ppermute | solution.py:165
  63.6 4.0 %collective-permute-done.9 = bf16[96,1024]{1,0:T(8,128)(2,1)S(1)} collective-permute-done((bf16[96,1024]{1,0:T(8,128)(2,1)S(1)}, bf16[96,1024]{1,0:T(8,128)(2,1)S(1)}, u32[]{:S(2)}, u32[]{:S(2)}) %collective-permute-start.9) | collective-permute-done | bytes 196640 | tf_op jit(solution)/shard_map/z_flood/ppermute | solution.py:176
  69.6 3.6 %collective-permute-done.10 = bf16[96,1024]{1,0:T(8,128)(2,1)S(1)} collective-permute-done((bf16[96,1024]{1,0:T(8,128)(2,1)S(1)}, bf16[96,1024]{1,0:T(8,128)(2,1)S(1)}, u32[]{:S(2)}, u32[]{:S(2)}) %collective-permute-start.10) | collective-permute-done | bytes 196640 | tf_op jit(solution)/shard_map/z_flood/ppermute | solution.py:176
  73.3 3.8 %collective-permute-done.8 = bf16[192,1024]{1,0:T(8,128)(2,1)} collective-permute-done((bf16[192,1024]{1,0:T(8,128)(2,1)S(1)}, bf16[192,1024]{1,0:T(8,128)(2,1)}, u32[]{:S(2)}, u32[]{:S(2)}) %collective-permute-start.8) | collective-permute-done | bytes 393248 | tf_op jit(solution)/shard_map/x_scatter_1/ppermute | solution.py:165
  77.1 6.7 %collective-permute-done.11.q1_ref = bf16[2,608,768]{2,1,0:T(8,128)(2,1)} collective-permute-done((bf16[2,608,768]{2,1,0:T(8,128)(2,1)S(1)}, bf16[2,608,768]{2,1,0:T(8,128)(2,1)}, u32[]{:S(2)}, u32[]{:S(2)}) %collective-permute-start.11) | collective-permute-done | bytes 1867808 | tf_op jit(solution)/shard_map/halo_y/ppermute | solution.py:211
  88.1 3.9 %collective-permute-start.13 = (bf16[2,96,1024]{2,1,0:T(8,128)(2,1)}, bf16[2,96,1024]{2,1,0:T(8,128)(2,1)S(1)}, u32[]{:S(2)}, u32[]{:S(2)}) collective-permute-start(bf16[2,96,1024]{2,1,0:T(8,128)(2,1)} %pad_maximum_fusion.1), channel_id=1, source_target_pairs={{0,56},{4,12},{8,0},{12,20},{16,8},{20,28},{24,16},{28,36},{32,24}... | collective-permute-start | bytes 1179656 | tf_op jit(solution)/shard_map/z_flood/ppermute | solution.py:176
  92.0 9.0 %collective-permute-done.12 = bf16[2,96,1024]{2,1,0:T(8,128)(2,1)S(1)} collective-permute-done((bf16[2,96,1024]{2,1,0:T(8,128)(2,1)}, bf16[2,96,1024]{2,1,0:T(8,128)(2,1)S(1)}, u32[]{:S(2)}, u32[]{:S(2)}) %collective-permute-start.12) | collective-permute-done | bytes 393248 | tf_op jit(solution)/shard_map/z_flood/ppermute | solution.py:176
  104.5 9.9 %collective-permute-done.14 = bf16[2,96,1024]{2,1,0:T(8,128)(2,1)} collective-permute-done((bf16[2,96,1024]{2,1,0:T(8,128)(2,1)S(1)}, bf16[2,96,1024]{2,1,0:T(8,128)(2,1)}, u32[]{:S(2)}, u32[]{:S(2)}) %collective-permute-start.14) | collective-permute-done | bytes 393248 | tf_op jit(solution)/shard_map/z_flood/ppermute | solution.py:176
  114.4 3.2 %collective-permute-start.18 = (bf16[2,96,1024]{2,1,0:T(8,128)(2,1)}, bf16[2,96,1024]{2,1,0:T(8,128)(2,1)}, u32[]{:S(2)}, u32[]{:S(2)}) collective-permute-start(bf16[2,96,1024]{2,1,0:T(8,128)(2,1)} %collective-permute-done.15), channel_id=1, source_target_pairs={{0,56},{4,12},{8,0},{12,20},{16,8},{20,28},{24,16},{28,36},{32,24}... | collective-permute-start | bytes 1179656 | tf_op jit(solution)/shard_map/z_flood/ppermute | solution.py:176
  118.5 8.3 %collective-permute-done.17 = bf16[2,96,1024]{2,1,0:T(8,128)(2,1)S(1)} collective-permute-done((bf16[2,96,1024]{2,1,0:T(8,128)(2,1)}, bf16[2,96,1024]{2,1,0:T(8,128)(2,1)S(1)}, u32[]{:S(2)}, u32[]{:S(2)}) %collective-permute-start.17) | collective-permute-done | bytes 393248 | tf_op jit(solution)/shard_map/z_flood/ppermute | solution.py:176
  142.2 5.3 %collective-permute-done.23.refs_3_ = bf16[192,1024]{1,0:T(8,128)(2,1)S(1)} collective-permute-done((bf16[192,1024]{1,0:T(8,128)(2,1)S(1)}, bf16[192,1024]{1,0:T(8,128)(2,1)S(1)}, u32[]{:S(2)}, u32[]{:S(2)}) %collective-permute-start.23) | collective-permute-done | bytes 393248 | tf_op jit(solution)/shard_map/x_gather_0/ppermute | solution.py:191
  147.5 7.0 %collective-permute-done.22.refs_2_ = bf16[192,1024]{1,0:T(8,128)(2,1)S(1)} collective-permute-done((bf16[192,1024]{1,0:T(8,128)(2,1)S(1)}, bf16[192,1024]{1,0:T(8,128)(2,1)S(1)}, u32[]{:S(2)}, u32[]{:S(2)}) %collective-permute-start.22) | collective-permute-done | bytes 393248 | tf_op jit(solution)/shard_map/x_gather_0/ppermute | solution.py:191
  158.1 10.1 %collective-permute-start.29 = (bf16[192,1024]{1,0:T(8,128)(2,1)S(1)}, bf16[192,1024]{1,0:T(8,128)(2,1)S(1)}, u32[]{:S(2)}, u32[]{:S(2)}) collective-permute-start(bf16[192,1024]{1,0:T(8,128)(2,1)S(1)} %pad_maximum_fusion.3.refs_0_), channel_id=1, source_target_pairs={{0,64},{4,196},{8,72},{12,204},{16,80},{20,212},{24,88},{28,220},{... | collective-permute-start | bytes 1179656 | tf_op jit(solution)/shard_map/x_gather_1/ppermute | solution.py:283
  171.3 10.0 %terms_0.1 = f32[2,8,128]{2,1,0:T(8,128)S(1)} custom-call(s32[10]{0:T(128)S(1)} %stack.61.place_ref, bf16[192,1024]{1,0:T(8,128)(2,1)S(1)} %pad_maximum_fusion.2.refs_0_, bf16[192,1024]{1,0:T(8,128)(2,1)} %collective-permute-done.21.refs_1_, bf16[192,1024]{1,0:T(8,128)(2,1)S(1)} %collective-permute-done.22.refs_2_, ...), custom_call_target="tpu_custom_call" | custom-call | flops 5737807872 | bytes 10616832 | tf_op jit(solution)/shard_map/terms_0/pallas_call | solution.py:75
  181.3 3.7 %collective-permute-start.31 = (bf16[192,1024]{1,0:T(8,128)(2,1)S(1)}, bf16[192,1024]{1,0:T(8,128)(2,1)S(1)}, u32[]{:S(2)}, u32[]{:S(2)}) collective-permute-start(bf16[192,1024]{1,0:T(8,128)(2,1)S(1)} %pad_maximum_fusion.3.refs_0_), channel_id=1, source_target_pairs={{0,128},{4,132},{8,136},{12,140},{16,144},{20,148},{24,152},{28,15... | collective-permute-start | bytes 1179656 | tf_op jit(solution)/shard_map/x_gather_1/ppermute | solution.py:285
  185.7 4.9 %branch.1 = bf16[2,2432,768]{2,1,0:T(8,128)(2,1)} custom-call(s32[8]{0:T(128)S(1)} %pad_add_fusion.plan_ref, bf16[2,2432,768]{2,1,0:T(8,128)(2,1)S(1)} %copy-done, bf16[2,2432,768]{2,1,0:T(8,128)(2,1)} %collective-permute-done.5.core_ref, bf16[2,608,768]{2,1,0:T(8,128)(2,1)S(1)} %collective-permute-done.4.q0_ref, ...), custom_call_target="tpu_custom_call" | custom-call | bytes 14942208 | tf_op jit(solution)/shard_map/branch/pallas_call | solution.py:132
  192.8 5.0 %collective-permute-done.30.refs_2_ = bf16[192,1024]{1,0:T(8,128)(2,1)S(1)} collective-permute-done((bf16[192,1024]{1,0:T(8,128)(2,1)S(1)}, bf16[192,1024]{1,0:T(8,128)(2,1)S(1)}, u32[]{:S(2)}, u32[]{:S(2)}) %collective-permute-start.30) | collective-permute-done | bytes 393248 | tf_op jit(solution)/shard_map/x_gather_1/ppermute | solution.py:285
  201.0 8.6 %terms_1.1 = f32[2,8,128]{2,1,0:T(8,128)S(1)} custom-call(s32[10]{0:T(128)S(1)} %stack.61.place_ref, bf16[192,1024]{1,0:T(8,128)(2,1)S(1)} %pad_maximum_fusion.3.refs_0_, bf16[192,1024]{1,0:T(8,128)(2,1)S(1)} %collective-permute-done.29.refs_1_, bf16[192,1024]{1,0:T(8,128)(2,1)S(1)} %collective-permute-done.30.refs_2_, ...), custom_call_target="tpu_custom_call" | custom-call | flops 5737807872 | bytes 10616832 | tf_op jit(solution)/shard_map/terms_1/pallas_call | solution.py:75
  214.4 3.5 %collective-permute-done.36 = f32[2,2]{1,0:T(2,128)S(1)} collective-permute-done((f32[2,2]{1,0:T(2,128)S(1)}, f32[2,2]{1,0:T(2,128)S(1)}, u32[]{:S(2)}, u32[]{:S(2)}) %collective-permute-start.36) | collective-permute-done | bytes 48 | tf_op jit(solution)/shard_map/results/ppermute | solution.py:296
  219.4 5.1 %collective-permute-done.39 = f32[2,6]{1,0:T(2,128)S(1)} collective-permute-done((f32[2,6]{1,0:T(2,128)S(1)}, f32[2,6]{1,0:T(2,128)S(1)}, u32[]{:S(2)}, u32[]{:S(2)}) %collective-permute-start.39) | collective-permute-done | bytes 80 | tf_op jit(solution)/shard_map/results/ppermute | solution.py:299
  (123 shorter events, 57.6 us)
Async XLA Ops:
  11.9 48.1 %collective-permute-start.5 = (bf16[2,2432,768]{2,1,0:T(8,128)(2,1)}, bf16[2,2432,768]{2,1,0:T(8,128)(2,1)}, u32[]{:S(2)}, u32[]{:S(2)}) collective-permute-start(bf16[2,2432,768]{2,1,0:T(8,128)(2,1)} %refs_8_.3), channel_id=1, source_target_pairs={{0,4},{4,0},{8,12},{12,8},{16,20},{20,16},{24,28},{28,24},{32,36},... | collective-permute-start | bytes 22413320 | tf_op jit(solution)/shard_map/core_walkers/ppermute | solution.py:195
  12.4 46.1 %collective-permute-start.4 = (bf16[2,608,768]{2,1,0:T(8,128)(2,1)}, bf16[2,608,768]{2,1,0:T(8,128)(2,1)S(1)}, u32[]{:S(2)}, u32[]{:S(2)}) collective-permute-start(bf16[2,608,768]{2,1,0:T(8,128)(2,1)} %constant_dynamic-slice_fusion), channel_id=1, source_target_pairs={{0,252},{4,8},{8,4},{12,16},{16,12},{20,24},{24,20},{28,32},{32,28... | collective-permute-start | bytes 5603336 | tf_op jit(solution)/shard_map/halo_z/ppermute | solution.py:221
  23.7 26.6 %collective-permute-start.3 = (bf16[192,1024]{1,0:T(8,128)(2,1)}, bf16[192,1024]{1,0:T(8,128)(2,1)S(1)}, u32[]{:S(2)}, u32[]{:S(2)}) collective-permute-start(bf16[192,1024]{1,0:T(8,128)(2,1)} %get-tuple-element.132), channel_id=1, source_target_pairs={{0,128},{4,132},{8,136},{12,140},{16,144},{20,148},{24,152},{28,15... | collective-permute-start | bytes 1179656 | tf_op jit(solution)/shard_map/x_scatter_0/ppermute | solution.py:165
  24.5 25.8 %collective-permute-start.2 = (bf16[192,1024]{1,0:T(8,128)(2,1)}, bf16[192,1024]{1,0:T(8,128)(2,1)}, u32[]{:S(2)}, u32[]{:S(2)}) collective-permute-start(bf16[192,1024]{1,0:T(8,128)(2,1)} %get-tuple-element.133), channel_id=1, source_target_pairs={{0,192},{4,68},{8,200},{12,76},{16,208},{20,84},{24,216},{28,92},{... | collective-permute-start | bytes 1179656 | tf_op jit(solution)/shard_map/x_scatter_0/ppermute | solution.py:165
  25.7 32.9 %collective-permute-start.1 = (bf16[192,1024]{1,0:T(8,128)(2,1)S(1)}, bf16[192,1024]{1,0:T(8,128)(2,1)}, u32[]{:S(2)}, u32[]{:S(2)}) collective-permute-start(bf16[192,1024]{1,0:T(8,128)(2,1)S(1)} %get-tuple-element.134), channel_id=1, source_target_pairs={{0,64},{4,196},{8,72},{12,204},{16,80},{20,212},{24,88},{28,220},{... | collective-permute-start | bytes 1179656 | tf_op jit(solution)/shard_map/x_scatter_0/ppermute | solution.py:165
  60.0 23.8 %collective-permute-start.11 = (bf16[2,608,768]{2,1,0:T(8,128)(2,1)S(1)}, bf16[2,608,768]{2,1,0:T(8,128)(2,1)}, u32[]{:S(2)}, u32[]{:S(2)}) collective-permute-start(bf16[2,608,768]{2,1,0:T(8,128)(2,1)S(1)} %collective-permute-done.4.q0_ref), channel_id=1, source_target_pairs={{0,1},{1,2},{2,3},{3,0},{4,7},{5,4},{6,5},{7,6},{8,9},{9,10},{10,1... | collective-permute-start | bytes 5603336 | tf_op jit(solution)/shard_map/halo_y/ppermute | solution.py:211
  60.4 12.9 %collective-permute-start.6 = (bf16[192,1024]{1,0:T(8,128)(2,1)}, bf16[192,1024]{1,0:T(8,128)(2,1)}, u32[]{:S(2)}, u32[]{:S(2)}) collective-permute-start(bf16[192,1024]{1,0:T(8,128)(2,1)} %get-tuple-element.80), channel_id=1, source_target_pairs={{0,64},{4,196},{8,72},{12,204},{16,80},{20,212},{24,88},{28,220},{... | collective-permute-start | bytes 1179656 | tf_op jit(solution)/shard_map/x_scatter_1/ppermute | solution.py:165
  60.4 12.9 %collective-permute-start.7 = (bf16[192,1024]{1,0:T(8,128)(2,1)}, bf16[192,1024]{1,0:T(8,128)(2,1)}, u32[]{:S(2)}, u32[]{:S(2)}) collective-permute-start(bf16[192,1024]{1,0:T(8,128)(2,1)} %get-tuple-element.81), channel_id=1, source_target_pairs={{0,192},{4,68},{8,200},{12,76},{16,208},{20,84},{24,216},{28,92},{... | collective-permute-start | bytes 1179656 | tf_op jit(solution)/shard_map/x_scatter_1/ppermute | solution.py:165
  63.6 13.5 %collective-permute-start.8 = (bf16[192,1024]{1,0:T(8,128)(2,1)S(1)}, bf16[192,1024]{1,0:T(8,128)(2,1)}, u32[]{:S(2)}, u32[]{:S(2)}) collective-permute-start(bf16[192,1024]{1,0:T(8,128)(2,1)S(1)} %get-tuple-element.82), channel_id=1, source_target_pairs={{0,128},{4,132},{8,136},{12,140},{16,144},{20,148},{24,152},{28,15... | collective-permute-start | bytes 1179656 | tf_op jit(solution)/shard_map/x_scatter_1/ppermute | solution.py:165
  83.8 30.6 %collective-permute-start.16 = (bf16[2,608,768]{2,1,0:T(8,128)(2,1)}, bf16[2,608,768]{2,1,0:T(8,128)(2,1)}, u32[]{:S(2)}, u32[]{:S(2)}) collective-permute-start(bf16[2,608,768]{2,1,0:T(8,128)(2,1)} %collective-permute-done.11.q1_ref), channel_id=1, source_target_pairs={{0,1},{1,2},{2,3},{3,0},{4,7},{5,4},{6,5},{7,6},{8,9},{9,10},{10,1... | collective-permute-start | bytes 5603336 | tf_op jit(solution)/shard_map/halo_y/ppermute | solution.py:211
  88.1 12.9 %collective-permute-start.12 = (bf16[2,96,1024]{2,1,0:T(8,128)(2,1)}, bf16[2,96,1024]{2,1,0:T(8,128)(2,1)S(1)}, u32[]{:S(2)}, u32[]{:S(2)}) collective-permute-start(bf16[2,96,1024]{2,1,0:T(8,128)(2,1)} %pad_maximum_fusion), channel_id=1, source_target_pairs={{0,8},{4,60},{8,16},{12,4},{16,24},{20,12},{24,32},{28,20},{32,40}... | collective-permute-start | bytes 1179656 | tf_op jit(solution)/shard_map/z_flood/ppermute | solution.py:176
  88.1 12.9 %collective-permute-start.13 = (bf16[2,96,1024]{2,1,0:T(8,128)(2,1)}, bf16[2,96,1024]{2,1,0:T(8,128)(2,1)S(1)}, u32[]{:S(2)}, u32[]{:S(2)}) collective-permute-start(bf16[2,96,1024]{2,1,0:T(8,128)(2,1)} %pad_maximum_fusion.1), channel_id=1, source_target_pairs={{0,56},{4,12},{8,0},{12,20},{16,8},{20,28},{24,16},{28,36},{32,24}... | collective-permute-start | bytes 1179656 | tf_op jit(solution)/shard_map/z_flood/ppermute | solution.py:176
  101.2 13.2 %collective-permute-start.14 = (bf16[2,96,1024]{2,1,0:T(8,128)(2,1)S(1)}, bf16[2,96,1024]{2,1,0:T(8,128)(2,1)}, u32[]{:S(2)}, u32[]{:S(2)}) collective-permute-start(bf16[2,96,1024]{2,1,0:T(8,128)(2,1)S(1)} %get-tuple-element.97), channel_id=1, source_target_pairs={{0,8},{4,60},{8,16},{12,4},{16,24},{20,12},{24,32},{28,20},{32,40}... | collective-permute-start | bytes 1179656 | tf_op jit(solution)/shard_map/z_flood/ppermute | solution.py:176
  101.3 13.1 %collective-permute-start.15 = (bf16[2,96,1024]{2,1,0:T(8,128)(2,1)S(1)}, bf16[2,96,1024]{2,1,0:T(8,128)(2,1)}, u32[]{:S(2)}, u32[]{:S(2)}) collective-permute-start(bf16[2,96,1024]{2,1,0:T(8,128)(2,1)S(1)} %get-tuple-element.98), channel_id=1, source_target_pairs={{0,56},{4,12},{8,0},{12,20},{16,8},{20,28},{24,16},{28,36},{32,24}... | collective-permute-start | bytes 1179656 | tf_op jit(solution)/shard_map/z_flood/ppermute | solution.py:176
  114.4 12.4 %collective-permute-start.17 = (bf16[2,96,1024]{2,1,0:T(8,128)(2,1)}, bf16[2,96,1024]{2,1,0:T(8,128)(2,1)S(1)}, u32[]{:S(2)}, u32[]{:S(2)}) collective-permute-start(bf16[2,96,1024]{2,1,0:T(8,128)(2,1)} %collective-permute-done.14), channel_id=1, source_target_pairs={{0,8},{4,60},{8,16},{12,4},{16,24},{20,12},{24,32},{28,20},{32,40}... | collective-permute-start | bytes 1179656 | tf_op jit(solution)/shard_map/z_flood/ppermute | solution.py:176
  114.4 12.4 %collective-permute-start.18 = (bf16[2,96,1024]{2,1,0:T(8,128)(2,1)}, bf16[2,96,1024]{2,1,0:T(8,128)(2,1)}, u32[]{:S(2)}, u32[]{:S(2)}) collective-permute-start(bf16[2,96,1024]{2,1,0:T(8,128)(2,1)} %collective-permute-done.15), channel_id=1, source_target_pairs={{0,56},{4,12},{8,0},{12,20},{16,8},{20,28},{24,16},{28,36},{32,24}... | collective-permute-start | bytes 1179656 | tf_op jit(solution)/shard_map/z_flood/ppermute | solution.py:176
  117.6 36.9 %collective-permute-start.24 = (bf16[2,608,768]{2,1,0:T(8,128)(2,1)}, bf16[2,608,768]{2,1,0:T(8,128)(2,1)}, u32[]{:S(2)}, u32[]{:S(2)}) collective-permute-start(bf16[2,608,768]{2,1,0:T(8,128)(2,1)} %collective-permute-done.16.q2_ref), channel_id=1, source_target_pairs={{0,1},{1,2},{2,3},{3,0},{4,7},{5,4},{6,5},{7,6},{8,9},{9,10},{10,1... | collective-permute-start | bytes 5603336 | tf_op jit(solution)/shard_map/halo_y/ppermute | solution.py:211
  133.9 13.6 %collective-permute-start.23 = (bf16[192,1024]{1,0:T(8,128)(2,1)S(1)}, bf16[192,1024]{1,0:T(8,128)(2,1)S(1)}, u32[]{:S(2)}, u32[]{:S(2)}) collective-permute-start(bf16[192,1024]{1,0:T(8,128)(2,1)S(1)} %pad_maximum_fusion.2.refs_0_), channel_id=1, source_target_pairs={{0,128},{4,132},{8,136},{12,140},{16,144},{20,148},{24,152},{28,15... | collective-permute-start | bytes 1179656 | tf_op jit(solution)/shard_map/x_gather_0/ppermute | solution.py:191
  135.6 18.8 %collective-permute-start.22 = (bf16[192,1024]{1,0:T(8,128)(2,1)S(1)}, bf16[192,1024]{1,0:T(8,128)(2,1)S(1)}, u32[]{:S(2)}, u32[]{:S(2)}) collective-permute-start(bf16[192,1024]{1,0:T(8,128)(2,1)S(1)} %pad_maximum_fusion.2.refs_0_), channel_id=1, source_target_pairs={{0,192},{4,68},{8,200},{12,76},{16,208},{20,84},{24,216},{28,92},{... | collective-permute-start | bytes 1179656 | tf_op jit(solution)/shard_map/x_gather_0/ppermute | solution.py:191
  138.6 15.9 %collective-permute-start.21 = (bf16[192,1024]{1,0:T(8,128)(2,1)S(1)}, bf16[192,1024]{1,0:T(8,128)(2,1)}, u32[]{:S(2)}, u32[]{:S(2)}) collective-permute-start(bf16[192,1024]{1,0:T(8,128)(2,1)S(1)} %pad_maximum_fusion.2.refs_0_), channel_id=1, source_target_pairs={{0,64},{4,196},{8,72},{12,204},{16,80},{20,212},{24,88},{28,220},{... | collective-permute-start | bytes 1179656 | tf_op jit(solution)/shard_map/x_gather_0/ppermute | solution.py:191
  158.1 23.3 %collective-permute-start.29 = (bf16[192,1024]{1,0:T(8,128)(2,1)S(1)}, bf16[192,1024]{1,0:T(8,128)(2,1)S(1)}, u32[]{:S(2)}, u32[]{:S(2)}) collective-permute-start(bf16[192,1024]{1,0:T(8,128)(2,1)S(1)} %pad_maximum_fusion.3.refs_0_), channel_id=1, source_target_pairs={{0,64},{4,196},{8,72},{12,204},{16,80},{20,212},{24,88},{28,220},{... | collective-permute-start | bytes 1179656 | tf_op jit(solution)/shard_map/x_gather_1/ppermute | solution.py:283
  181.3 16.5 %collective-permute-start.31 = (bf16[192,1024]{1,0:T(8,128)(2,1)S(1)}, bf16[192,1024]{1,0:T(8,128)(2,1)S(1)}, u32[]{:S(2)}, u32[]{:S(2)}) collective-permute-start(bf16[192,1024]{1,0:T(8,128)(2,1)S(1)} %pad_maximum_fusion.3.refs_0_), channel_id=1, source_target_pairs={{0,128},{4,132},{8,136},{12,140},{16,144},{20,148},{24,152},{28,15... | collective-permute-start | bytes 1179656 | tf_op jit(solution)/shard_map/x_gather_1/ppermute | solution.py:285
  185.1 12.8 %collective-permute-start.30 = (bf16[192,1024]{1,0:T(8,128)(2,1)S(1)}, bf16[192,1024]{1,0:T(8,128)(2,1)S(1)}, u32[]{:S(2)}, u32[]{:S(2)}) collective-permute-start(bf16[192,1024]{1,0:T(8,128)(2,1)S(1)} %pad_maximum_fusion.3.refs_0_), channel_id=1, source_target_pairs={{0,192},{4,68},{8,200},{12,76},{16,208},{20,84},{24,216},{28,92},{... | collective-permute-start | bytes 1179656 | tf_op jit(solution)/shard_map/x_gather_1/ppermute | solution.py:285
  185.6 13.5 %collective-permute-start.32 = (bf16[192,1024]{1,0:T(8,128)(2,1)S(1)}, bf16[192,1024]{1,0:T(8,128)(2,1)S(1)}, u32[]{:S(2)}, u32[]{:S(2)}) collective-permute-start(bf16[192,1024]{1,0:T(8,128)(2,1)S(1)} %pad_maximum_fusion.3.refs_0_), channel_id=1, source_target_pairs={{0,4},{4,0},{8,12},{12,8},{16,20},{20,16},{24,28},{28,24},{32,36},... | collective-permute-start | bytes 1179656 | tf_op jit(solution)/shard_map/core_gather_1/ppermute | solution.py:195
  (29 other events, 259.9 us)
where the time goes:
time: 230 us; the launch traced here: 226 us
  waiting for transfers between devices  111 us (48%)
  starting transfers between devices  58 us (25%)
  Pallas kernels  23.5 us (10%)
  other arithmetic  14.1 us (6%)
  local copies, waits for them, and re-layouts  13 us (6%)
  between operations  6.38 us (3%)
    ppermute x6, waiting for transfers between devices, scatter(): lax.ppermute(sent, 'walk', to_chip(dx, 0))  35.8 us
    ppermute x5, waiting for transfers between devices, flood_step(): lax.ppermute(up, 'walk', to_chip(0, 1))  31.5 us
    pallas_call x2, Pallas kernels, walker_terms(): pl.pallas_call(terms_kernel, grid_spec=pltpu.PrefetchScalarGridSpec(num_s...  18.6 us
    ppermute x5, starting transfers between devices, flood_step(): lax.ppermute(down, 'walk', to_chip(0, -1))  12.6 us
    ppermute x3, waiting for transfers between devices, along_x(): return [lax.ppermute(piece, 'walk', to_chip(dx, 0)) for dx in (1, 3, 2)]  12.3 us
    ppermute x1, starting transfers between devices, shards(): ahead = lax.ppermute(piece, 'walk', to_chip(1, 0))  10.1 us
    ppermute x1, starting transfers between devices, shards(): quarters = [lax.ppermute(quarter, 'walk', across_chips())]  7.68 us
    ppermute x3, waiting for transfers between devices, pass_on(): return lax.ppermute(quarter, ('walk', 'vec'), both_ways)  6.75 us
  transfers between devices with their start and end apart: 41, of which 24 were waited for; matrix products, arithmetic and copies ran while one was open for 9% of the time, Pallas kernels for 7%

commit v1 on v0

--- a/solution.py
+++ b/solution.py
@@ -85,7 +85,7 @@
             ],
         ),
         out_shape=jax.ShapeDtypeStruct((count, 8, 128), jnp.float32),
-        compiler_params=pltpu.CompilerParams(vmem_limit_bytes=40 * 2**20),
+        compiler_params=pltpu.CompilerParams(vmem_limit_bytes=50 * 2**20),
         cost_estimate=pl.CostEstimate(
             flops=2 * count * electrons * (2 * NX * depth // 2 + width) * width,
             bytes_accessed=2 * (len(pieces) * pieces[0].size + walkers.size),
@@ -232,7 +232,8 @@
 
     with jax.named_scope("x_scatter_0"):
         arrived = scatter(blocks[0])
-        arrived, sent, quarters[0] = after((arrived, blocks[1], quarters[0]))
+        arrived, sent, quarters[0] = after((arrived[::-1], blocks[1], quarters[0]))
+        arrived = arrived[::-1]
         piece = scattered(blocks[0][0], arrived, owner_x[0], x, c)
         halves = [(piece[:half], piece[half:])]
         halves[0], sent, quarters[0], other_core = after((halves[0], sent, quarters[0], other_core))
@@ -265,7 +266,8 @@
         mine = [piece] + along_x(piece)
     with jax.named_scope("z_flood"):
         piece = flooded(halves[1], [[a[1] for a in b] for b in (second, third, fourth)] + [fifth], away[1])
-        piece, mine, quarters[3] = after((piece, mine, quarters[3]))
+        piece, mine, quarters[3] = after((piece, mine[::-1], quarters[3]))
+        mine = mine[::-1]
     with jax.named_scope("core_gather_0"):
         pieces = mine + [to_other_core(p) for p in mine]
         piece, pieces = after((piece, pieces))

time: 230 us -> 231 us (level)
  Pallas kernels: 23.5 us -> 28.2 us
  starting transfers between devices: 58 us -> 55.3 us
    pallas_call x2, Pallas kernels: 18.6 us -> 21.8 us  [walker_terms(): pl.pallas_call(terms_kernel, grid_spec=pltpu.PrefetchScalarGridSpec(num_s...]
    unnamed x24 -> x26, local copies, waits for them, and re-layouts: 4.82 us -> 2.56 us
  transfers between devices with their start and end apart: 41 -> 41, of which waited for: 24 -> 24; matrix products, arithmetic and copies ran while one was open for 9% -> 9% of each run, Pallas kernels for 7% -> 8%
where the time goes in v1:
time: 231 us; the launch traced here: 226 us
  waiting for transfers between devices  113 us (49%)
  starting transfers between devices  55.3 us (24%)
  Pallas kernels  28.2 us (12%)
  other arithmetic  13 us (6%)
  local copies, waits for them, and re-layouts  10.7 us (5%)
  between operations  6.41 us (3%)
    ppermute x6, waiting for transfers between devices, scatter(): lax.ppermute(sent, 'walk', to_chip(dx, 0))  36.2 us
    ppermute x5, waiting for transfers between devices, flood_step(): lax.ppermute(up, 'walk', to_chip(0, 1))  31.4 us
    pallas_call x2, Pallas kernels, walker_terms(): pl.pallas_call(terms_kernel, grid_spec=pltpu.PrefetchScalarGridSpec(num_s...  21.8 us
    ppermute x3, waiting for transfers between devices, along_x(): return [lax.ppermute(piece, 'walk', to_chip(dx, 0)) for dx in (1, 3, 2)]  13.3 us
    ppermute x5, starting transfers between devices, flood_step(): lax.ppermute(down, 'walk', to_chip(0, -1))  11.4 us
    ppermute x1, starting transfers between devices, shards(): ahead = lax.ppermute(piece, 'walk', to_chip(1, 0))  9.81 us
    ppermute x1, starting transfers between devices, shards(): quarters = [lax.ppermute(quarter, 'walk', across_chips())]  7.68 us
    ppermute x6, starting transfers between devices, scatter(): lax.ppermute(sent, 'walk', to_chip(dx, 0))  6.48 us
  transfers between devices with their start and end apart: 41, of which 24 were waited for; matrix products, arithmetic and copies ran while one was open for 9% of the time, Pallas kernels for 8%

profile of v1, /device:TPU:24, one launch (start us, length us, event | category | flops | bytes accessed | tf_op | source)
XLA Modules:
  0.0 226.5 jit_solution(10750412301408010197)
XLA Ops:
  12.4 7.7 %collective-permute-start.4 = (bf16[2,608,768]{2,1,0:T(8,128)(2,1)}, bf16[2,608,768]{2,1,0:T(8,128)(2,1)S(1)}, u32[]{:S(2)}, u32[]{:S(2)}) collective-permute-start(bf16[2,608,768]{2,1,0:T(8,128)(2,1)} %constant_dynamic-slice_fusion), channel_id=1, source_target_pairs={{0,252},{4,8},{8,4},{12,16},{16,12},{20,24},{24,20},{28,32},{32,28... | collective-permute-start | bytes 5603336 | tf_op jit(solution)/shard_map/halo_z/ppermute | solution.py:221
  20.1 3.7 %bitcast_select_fusion.6 = (bf16[192,1024]{1,0:T(8,128)(2,1)S(1)}, bf16[192,1024]{1,0:T(8,128)(2,1)}, bf16[192,1024]{1,0:T(8,128)(2,1)}, bf16[192,1024]{1,0:T(8,...) fusion(pred[]{:T(512)S(6)} %eq.185, ...), kind=kLoop, calls=%fused_computation.13 | loop fusion | flops 1376256 | bytes 5898262 | tf_op jit(solution)/shard_map/blocks/jit(_where)/select_n | solution.py:159
  23.8 3.2 %collective-permute-start.2 = (bf16[192,1024]{1,0:T(8,128)(2,1)}, bf16[192,1024]{1,0:T(8,128)(2,1)}, u32[]{:S(2)}, u32[]{:S(2)}) collective-permute-start(bf16[192,1024]{1,0:T(8,128)(2,1)} %get-tuple-element.133), channel_id=1, source_target_pairs={{0,192},{4,68},{8,200},{12,76},{16,208},{20,84},{24,216},{28,92},{... | collective-permute-start | bytes 1179656 | tf_op jit(solution)/shard_map/x_scatter_0/ppermute | solution.py:165
  27.0 23.0 %collective-permute-done.3 = bf16[192,1024]{1,0:T(8,128)(2,1)S(1)} collective-permute-done((bf16[192,1024]{1,0:T(8,128)(2,1)}, bf16[192,1024]{1,0:T(8,128)(2,1)S(1)}, u32[]{:S(2)}, u32[]{:S(2)}) %collective-permute-start.3) | collective-permute-done | bytes 393248 | tf_op jit(solution)/shard_map/x_scatter_0/ppermute | solution.py:165
  50.0 8.8 %collective-permute-done.1 = bf16[192,1024]{1,0:T(8,128)(2,1)} collective-permute-done((bf16[192,1024]{1,0:T(8,128)(2,1)S(1)}, bf16[192,1024]{1,0:T(8,128)(2,1)}, u32[]{:S(2)}, u32[]{:S(2)}) %collective-permute-start.1) | collective-permute-done | bytes 393248 | tf_op jit(solution)/shard_map/x_scatter_0/ppermute | solution.py:165
  60.7 3.2 %collective-permute-start.7 = (bf16[192,1024]{1,0:T(8,128)(2,1)}, bf16[192,1024]{1,0:T(8,128)(2,1)}, u32[]{:S(2)}, u32[]{:S(2)}) collective-permute-start(bf16[192,1024]{1,0:T(8,128)(2,1)} %get-tuple-element.81), channel_id=1, source_target_pairs={{0,192},{4,68},{8,200},{12,76},{16,208},{20,84},{24,216},{28,92},{... | collective-permute-start | bytes 1179656 | tf_op jit(solution)/shard_map/x_scatter_1/ppermute | solution.py:165
  64.0 3.6 %collective-permute-done.9 = bf16[96,1024]{1,0:T(8,128)(2,1)S(1)} collective-permute-done((bf16[96,1024]{1,0:T(8,128)(2,1)S(1)}, bf16[96,1024]{1,0:T(8,128)(2,1)S(1)}, u32[]{:S(2)}, u32[]{:S(2)}) %collective-permute-start.9) | collective-permute-done | bytes 196640 | tf_op jit(solution)/shard_map/z_flood/ppermute | solution.py:176
  68.7 4.6 %collective-permute-done.10 = bf16[96,1024]{1,0:T(8,128)(2,1)S(1)} collective-permute-done((bf16[96,1024]{1,0:T(8,128)(2,1)S(1)}, bf16[96,1024]{1,0:T(8,128)(2,1)S(1)}, u32[]{:S(2)}, u32[]{:S(2)}) %collective-permute-start.10) | collective-permute-done | bytes 196640 | tf_op jit(solution)/shard_map/z_flood/ppermute | solution.py:176
  73.4 4.3 %collective-permute-done.8 = bf16[192,1024]{1,0:T(8,128)(2,1)} collective-permute-done((bf16[192,1024]{1,0:T(8,128)(2,1)S(1)}, bf16[192,1024]{1,0:T(8,128)(2,1)}, u32[]{:S(2)}, u32[]{:S(2)}) %collective-permute-start.8) | collective-permute-done | bytes 393248 | tf_op jit(solution)/shard_map/x_scatter_1/ppermute | solution.py:165
  77.7 6.4 %collective-permute-done.11.q1_ref = bf16[2,608,768]{2,1,0:T(8,128)(2,1)} collective-permute-done((bf16[2,608,768]{2,1,0:T(8,128)(2,1)S(1)}, bf16[2,608,768]{2,1,0:T(8,128)(2,1)}, u32[]{:S(2)}, u32[]{:S(2)}) %collective-permute-start.11) | collective-permute-done | bytes 1867808 | tf_op jit(solution)/shard_map/halo_y/ppermute | solution.py:211
  88.3 3.5 %collective-permute-start.13 = (bf16[2,96,1024]{2,1,0:T(8,128)(2,1)}, bf16[2,96,1024]{2,1,0:T(8,128)(2,1)S(1)}, u32[]{:S(2)}, u32[]{:S(2)}) collective-permute-start(bf16[2,96,1024]{2,1,0:T(8,128)(2,1)} %pad_maximum_fusion.1), channel_id=1, source_target_pairs={{0,56},{4,12},{8,0},{12,20},{16,8},{20,28},{24,16},{28,36},{32,24}... | collective-permute-start | bytes 1179656 | tf_op jit(solution)/shard_map/z_flood/ppermute | solution.py:176
  91.8 9.3 %collective-permute-done.12 = bf16[2,96,1024]{2,1,0:T(8,128)(2,1)S(1)} collective-permute-done((bf16[2,96,1024]{2,1,0:T(8,128)(2,1)}, bf16[2,96,1024]{2,1,0:T(8,128)(2,1)S(1)}, u32[]{:S(2)}, u32[]{:S(2)}) %collective-permute-start.12) | collective-permute-done | bytes 393248 | tf_op jit(solution)/shard_map/z_flood/ppermute | solution.py:176
  104.6 9.5 %collective-permute-done.14 = bf16[2,96,1024]{2,1,0:T(8,128)(2,1)} collective-permute-done((bf16[2,96,1024]{2,1,0:T(8,128)(2,1)S(1)}, bf16[2,96,1024]{2,1,0:T(8,128)(2,1)}, u32[]{:S(2)}, u32[]{:S(2)}) %collective-permute-start.14) | collective-permute-done | bytes 393248 | tf_op jit(solution)/shard_map/z_flood/ppermute | solution.py:176
  117.4 8.9 %collective-permute-done.17 = bf16[2,96,1024]{2,1,0:T(8,128)(2,1)S(1)} collective-permute-done((bf16[2,96,1024]{2,1,0:T(8,128)(2,1)}, bf16[2,96,1024]{2,1,0:T(8,128)(2,1)S(1)}, u32[]{:S(2)}, u32[]{:S(2)}) %collective-permute-start.17) | collective-permute-done | bytes 393248 | tf_op jit(solution)/shard_map/z_flood/ppermute | solution.py:176
  141.8 3.2 %collective-permute-done.23.refs_1_ = bf16[192,1024]{1,0:T(8,128)(2,1)S(1)} collective-permute-done((bf16[192,1024]{1,0:T(8,128)(2,1)S(1)}, bf16[192,1024]{1,0:T(8,128)(2,1)S(1)}, u32[]{:S(2)}, u32[]{:S(2)}) %collective-permute-start.23) | collective-permute-done | bytes 393248 | tf_op jit(solution)/shard_map/x_gather_0/ppermute | solution.py:191
  145.1 8.1 %collective-permute-done.22.refs_2_ = bf16[192,1024]{1,0:T(8,128)(2,1)S(1)} collective-permute-done((bf16[192,1024]{1,0:T(8,128)(2,1)S(1)}, bf16[192,1024]{1,0:T(8,128)(2,1)S(1)}, u32[]{:S(2)}, u32[]{:S(2)}) %collective-permute-start.22) | collective-permute-done | bytes 393248 | tf_op jit(solution)/shard_map/x_gather_0/ppermute | solution.py:191
  158.7 9.8 %collective-permute-start.29 = (bf16[192,1024]{1,0:T(8,128)(2,1)S(1)}, bf16[192,1024]{1,0:T(8,128)(2,1)S(1)}, u32[]{:S(2)}, u32[]{:S(2)}) collective-permute-start(bf16[192,1024]{1,0:T(8,128)(2,1)S(1)} %pad_maximum_fusion.3.refs_0_), channel_id=1, source_target_pairs={{0,64},{4,196},{8,72},{12,204},{16,80},{20,212},{24,88},{28,220},{... | collective-permute-start | bytes 1179656 | tf_op jit(solution)/shard_map/x_gather_1/ppermute | solution.py:285
  168.5 11.2 %terms_0.1 = f32[2,8,128]{2,1,0:T(8,128)S(1)} custom-call(s32[10]{0:T(128)S(1)} %stack.61.place_ref, bf16[192,1024]{1,0:T(8,128)(2,1)S(1)} %pad_maximum_fusion.2.refs_0_, bf16[192,1024]{1,0:T(8,128)(2,1)S(1)} %collective-permute-done.23.refs_1_, bf16[192,1024]{1,0:T(8,128)(2,1)S(1)} %collective-permute-done.22.refs_2_, ...), custom_call_target="tpu_custom_call" | custom-call | flops 5737807872 | bytes 10616832 | tf_op jit(solution)/shard_map/terms_0/pallas_call | solution.py:75
  179.7 3.4 %collective-permute-start.31 = (bf16[192,1024]{1,0:T(8,128)(2,1)S(1)}, bf16[192,1024]{1,0:T(8,128)(2,1)S(1)}, u32[]{:S(2)}, u32[]{:S(2)}) collective-permute-start(bf16[192,1024]{1,0:T(8,128)(2,1)S(1)} %pad_maximum_fusion.3.refs_0_), channel_id=1, source_target_pairs={{0,128},{4,132},{8,136},{12,140},{16,144},{20,148},{24,152},{28,15... | collective-permute-start | bytes 1179656 | tf_op jit(solution)/shard_map/x_gather_1/ppermute | solution.py:287
  184.6 6.4 %branch.1 = bf16[2,2432,768]{2,1,0:T(8,128)(2,1)} custom-call(s32[8]{0:T(128)S(1)} %pad_add_fusion.plan_ref, bf16[2,2432,768]{2,1,0:T(8,128)(2,1)S(1)} %bitcast.135, bf16[2,2432,768]{2,1,0:T(8,128)(2,1)} %collective-permute-done.5.core_ref, bf16[2,608,768]{2,1,0:T(8,128)(2,1)S(1)} %collective-permute-done.4.q0_ref, ...), custom_call_target="tpu_custom_call" | custom-call | bytes 14942208 | tf_op jit(solution)/shard_map/branch/pallas_call | solution.py:132
  191.7 4.7 %collective-permute-done.30.refs_2_ = bf16[192,1024]{1,0:T(8,128)(2,1)S(1)} collective-permute-done((bf16[192,1024]{1,0:T(8,128)(2,1)S(1)}, bf16[192,1024]{1,0:T(8,128)(2,1)S(1)}, u32[]{:S(2)}, u32[]{:S(2)}) %collective-permute-start.30) | collective-permute-done | bytes 393248 | tf_op jit(solution)/shard_map/x_gather_1/ppermute | solution.py:287
  199.3 10.6 %terms_1.1 = f32[2,8,128]{2,1,0:T(8,128)S(1)} custom-call(s32[10]{0:T(128)S(1)} %stack.61.place_ref, bf16[192,1024]{1,0:T(8,128)(2,1)S(1)} %pad_maximum_fusion.3.refs_0_, bf16[192,1024]{1,0:T(8,128)(2,1)S(1)} %collective-permute-done.29.refs_1_, bf16[192,1024]{1,0:T(8,128)(2,1)S(1)} %collective-permute-done.30.refs_2_, ...), custom_call_target="tpu_custom_call" | custom-call | flops 5737807872 | bytes 10616832 | tf_op jit(solution)/shard_map/terms_1/pallas_call | solution.py:75
  214.8 3.5 %collective-permute-done.36 = f32[2,2]{1,0:T(2,128)S(1)} collective-permute-done((f32[2,2]{1,0:T(2,128)S(1)}, f32[2,2]{1,0:T(2,128)S(1)}, u32[]{:S(2)}, u32[]{:S(2)}) %collective-permute-start.36) | collective-permute-done | bytes 48 | tf_op jit(solution)/shard_map/results/ppermute | solution.py:298
  219.7 5.1 %collective-permute-done.39 = f32[2,6]{1,0:T(2,128)S(1)} collective-permute-done((f32[2,6]{1,0:T(2,128)S(1)}, f32[2,6]{1,0:T(2,128)S(1)}, u32[]{:S(2)}, u32[]{:S(2)}) %collective-permute-start.39) | collective-permute-done | bytes 80 | tf_op jit(solution)/shard_map/results/ppermute | solution.py:301
  (126 shorter events, 54.3 us)
Async XLA Ops:
  11.9 48.4 %collective-permute-start.5 = (bf16[2,2432,768]{2,1,0:T(8,128)(2,1)}, bf16[2,2432,768]{2,1,0:T(8,128)(2,1)}, u32[]{:S(2)}, u32[]{:S(2)}) collective-permute-start(bf16[2,2432,768]{2,1,0:T(8,128)(2,1)} %refs_8_.3), channel_id=1, source_target_pairs={{0,4},{4,0},{8,12},{12,8},{16,20},{20,16},{24,28},{28,24},{32,36},... | collective-permute-start | bytes 22413320 | tf_op jit(solution)/shard_map/core_walkers/ppermute | solution.py:195
  12.4 46.4 %collective-permute-start.4 = (bf16[2,608,768]{2,1,0:T(8,128)(2,1)}, bf16[2,608,768]{2,1,0:T(8,128)(2,1)S(1)}, u32[]{:S(2)}, u32[]{:S(2)}) collective-permute-start(bf16[2,608,768]{2,1,0:T(8,128)(2,1)} %constant_dynamic-slice_fusion), channel_id=1, source_target_pairs={{0,252},{4,8},{8,4},{12,16},{16,12},{20,24},{24,20},{28,32},{32,28... | collective-permute-start | bytes 5603336 | tf_op jit(solution)/shard_map/halo_z/ppermute | solution.py:221
  23.7 26.2 %collective-permute-start.3 = (bf16[192,1024]{1,0:T(8,128)(2,1)}, bf16[192,1024]{1,0:T(8,128)(2,1)S(1)}, u32[]{:S(2)}, u32[]{:S(2)}) collective-permute-start(bf16[192,1024]{1,0:T(8,128)(2,1)} %get-tuple-element.132), channel_id=1, source_target_pairs={{0,64},{4,196},{8,72},{12,204},{16,80},{20,212},{24,88},{28,220},{... | collective-permute-start | bytes 1179656 | tf_op jit(solution)/shard_map/x_scatter_0/ppermute | solution.py:165
  23.8 26.2 %collective-permute-start.2 = (bf16[192,1024]{1,0:T(8,128)(2,1)}, bf16[192,1024]{1,0:T(8,128)(2,1)}, u32[]{:S(2)}, u32[]{:S(2)}) collective-permute-start(bf16[192,1024]{1,0:T(8,128)(2,1)} %get-tuple-element.133), channel_id=1, source_target_pairs={{0,192},{4,68},{8,200},{12,76},{16,208},{20,84},{24,216},{28,92},{... | collective-permute-start | bytes 1179656 | tf_op jit(solution)/shard_map/x_scatter_0/ppermute | solution.py:165
  27.0 31.8 %collective-permute-start.1 = (bf16[192,1024]{1,0:T(8,128)(2,1)S(1)}, bf16[192,1024]{1,0:T(8,128)(2,1)}, u32[]{:S(2)}, u32[]{:S(2)}) collective-permute-start(bf16[192,1024]{1,0:T(8,128)(2,1)S(1)} %get-tuple-element.134), channel_id=1, source_target_pairs={{0,128},{4,132},{8,136},{12,140},{16,144},{20,148},{24,152},{28,15... | collective-permute-start | bytes 1179656 | tf_op jit(solution)/shard_map/x_scatter_0/ppermute | solution.py:165
  60.3 23.8 %collective-permute-start.11 = (bf16[2,608,768]{2,1,0:T(8,128)(2,1)S(1)}, bf16[2,608,768]{2,1,0:T(8,128)(2,1)}, u32[]{:S(2)}, u32[]{:S(2)}) collective-permute-start(bf16[2,608,768]{2,1,0:T(8,128)(2,1)S(1)} %collective-permute-done.4.q0_ref), channel_id=1, source_target_pairs={{0,1},{1,2},{2,3},{3,0},{4,7},{5,4},{6,5},{7,6},{8,9},{9,10},{10,1... | collective-permute-start | bytes 5603336 | tf_op jit(solution)/shard_map/halo_y/ppermute | solution.py:211
  60.7 12.6 %collective-permute-start.6 = (bf16[192,1024]{1,0:T(8,128)(2,1)}, bf16[192,1024]{1,0:T(8,128)(2,1)}, u32[]{:S(2)}, u32[]{:S(2)}) collective-permute-start(bf16[192,1024]{1,0:T(8,128)(2,1)} %get-tuple-element.80), channel_id=1, source_target_pairs={{0,64},{4,196},{8,72},{12,204},{16,80},{20,212},{24,88},{28,220},{... | collective-permute-start | bytes 1179656 | tf_op jit(solution)/shard_map/x_scatter_1/ppermute | solution.py:165
  60.7 12.7 %collective-permute-start.7 = (bf16[192,1024]{1,0:T(8,128)(2,1)}, bf16[192,1024]{1,0:T(8,128)(2,1)}, u32[]{:S(2)}, u32[]{:S(2)}) collective-permute-start(bf16[192,1024]{1,0:T(8,128)(2,1)} %get-tuple-element.81), channel_id=1, source_target_pairs={{0,192},{4,68},{8,200},{12,76},{16,208},{20,84},{24,216},{28,92},{... | collective-permute-start | bytes 1179656 | tf_op jit(solution)/shard_map/x_scatter_1/ppermute | solution.py:165
  64.0 13.7 %collective-permute-start.8 = (bf16[192,1024]{1,0:T(8,128)(2,1)S(1)}, bf16[192,1024]{1,0:T(8,128)(2,1)}, u32[]{:S(2)}, u32[]{:S(2)}) collective-permute-start(bf16[192,1024]{1,0:T(8,128)(2,1)S(1)} %get-tuple-element.82), channel_id=1, source_target_pairs={{0,128},{4,132},{8,136},{12,140},{16,144},{20,148},{24,152},{28,15... | collective-permute-start | bytes 1179656 | tf_op jit(solution)/shard_map/x_scatter_1/ppermute | solution.py:165
  84.1 30.1 %collective-permute-start.16 = (bf16[2,608,768]{2,1,0:T(8,128)(2,1)}, bf16[2,608,768]{2,1,0:T(8,128)(2,1)}, u32[]{:S(2)}, u32[]{:S(2)}) collective-permute-start(bf16[2,608,768]{2,1,0:T(8,128)(2,1)} %collective-permute-done.11.q1_ref), channel_id=1, source_target_pairs={{0,1},{1,2},{2,3},{3,0},{4,7},{5,4},{6,5},{7,6},{8,9},{9,10},{10,1... | collective-permute-start | bytes 5603336 | tf_op jit(solution)/shard_map/halo_y/ppermute | solution.py:211
  88.3 12.9 %collective-permute-start.12 = (bf16[2,96,1024]{2,1,0:T(8,128)(2,1)}, bf16[2,96,1024]{2,1,0:T(8,128)(2,1)S(1)}, u32[]{:S(2)}, u32[]{:S(2)}) collective-permute-start(bf16[2,96,1024]{2,1,0:T(8,128)(2,1)} %pad_maximum_fusion), channel_id=1, source_target_pairs={{0,8},{4,60},{8,16},{12,4},{16,24},{20,12},{24,32},{28,20},{32,40}... | collective-permute-start | bytes 1179656 | tf_op jit(solution)/shard_map/z_flood/ppermute | solution.py:176
  88.3 12.9 %collective-permute-start.13 = (bf16[2,96,1024]{2,1,0:T(8,128)(2,1)}, bf16[2,96,1024]{2,1,0:T(8,128)(2,1)S(1)}, u32[]{:S(2)}, u32[]{:S(2)}) collective-permute-start(bf16[2,96,1024]{2,1,0:T(8,128)(2,1)} %pad_maximum_fusion.1), channel_id=1, source_target_pairs={{0,56},{4,12},{8,0},{12,20},{16,8},{20,28},{24,16},{28,36},{32,24}... | collective-permute-start | bytes 1179656 | tf_op jit(solution)/shard_map/z_flood/ppermute | solution.py:176
  101.3 12.9 %collective-permute-start.14 = (bf16[2,96,1024]{2,1,0:T(8,128)(2,1)S(1)}, bf16[2,96,1024]{2,1,0:T(8,128)(2,1)}, u32[]{:S(2)}, u32[]{:S(2)}) collective-permute-start(bf16[2,96,1024]{2,1,0:T(8,128)(2,1)S(1)} %get-tuple-element.97), channel_id=1, source_target_pairs={{0,8},{4,60},{8,16},{12,4},{16,24},{20,12},{24,32},{28,20},{32,40}... | collective-permute-start | bytes 1179656 | tf_op jit(solution)/shard_map/z_flood/ppermute | solution.py:176
  101.4 12.8 %collective-permute-start.15 = (bf16[2,96,1024]{2,1,0:T(8,128)(2,1)S(1)}, bf16[2,96,1024]{2,1,0:T(8,128)(2,1)}, u32[]{:S(2)}, u32[]{:S(2)}) collective-permute-start(bf16[2,96,1024]{2,1,0:T(8,128)(2,1)S(1)} %get-tuple-element.98), channel_id=1, source_target_pairs={{0,56},{4,12},{8,0},{12,20},{16,8},{20,28},{24,16},{28,36},{32,24}... | collective-permute-start | bytes 1179656 | tf_op jit(solution)/shard_map/z_flood/ppermute | solution.py:176
  114.2 12.1 %collective-permute-start.17 = (bf16[2,96,1024]{2,1,0:T(8,128)(2,1)}, bf16[2,96,1024]{2,1,0:T(8,128)(2,1)S(1)}, u32[]{:S(2)}, u32[]{:S(2)}) collective-permute-start(bf16[2,96,1024]{2,1,0:T(8,128)(2,1)} %collective-permute-done.14), channel_id=1, source_target_pairs={{0,8},{4,60},{8,16},{12,4},{16,24},{20,12},{24,32},{28,20},{32,40}... | collective-permute-start | bytes 1179656 | tf_op jit(solution)/shard_map/z_flood/ppermute | solution.py:176
  114.2 12.1 %collective-permute-start.18 = (bf16[2,96,1024]{2,1,0:T(8,128)(2,1)}, bf16[2,96,1024]{2,1,0:T(8,128)(2,1)}, u32[]{:S(2)}, u32[]{:S(2)}) collective-permute-start(bf16[2,96,1024]{2,1,0:T(8,128)(2,1)} %collective-permute-done.15), channel_id=1, source_target_pairs={{0,56},{4,12},{8,0},{12,20},{16,8},{20,28},{24,16},{28,36},{32,24}... | collective-permute-start | bytes 1179656 | tf_op jit(solution)/shard_map/z_flood/ppermute | solution.py:176
  117.4 37.8 %collective-permute-start.24 = (bf16[2,608,768]{2,1,0:T(8,128)(2,1)}, bf16[2,608,768]{2,1,0:T(8,128)(2,1)}, u32[]{:S(2)}, u32[]{:S(2)}) collective-permute-start(bf16[2,608,768]{2,1,0:T(8,128)(2,1)} %collective-permute-done.16.q2_ref), channel_id=1, source_target_pairs={{0,1},{1,2},{2,3},{3,0},{4,7},{5,4},{6,5},{7,6},{8,9},{9,10},{10,1... | collective-permute-start | bytes 5603336 | tf_op jit(solution)/shard_map/halo_y/ppermute | solution.py:211
  133.4 11.6 %collective-permute-start.23 = (bf16[192,1024]{1,0:T(8,128)(2,1)S(1)}, bf16[192,1024]{1,0:T(8,128)(2,1)S(1)}, u32[]{:S(2)}, u32[]{:S(2)}) collective-permute-start(bf16[192,1024]{1,0:T(8,128)(2,1)S(1)} %pad_maximum_fusion.2.refs_0_), channel_id=1, source_target_pairs={{0,64},{4,196},{8,72},{12,204},{16,80},{20,212},{24,88},{28,220},{... | collective-permute-start | bytes 1179656 | tf_op jit(solution)/shard_map/x_gather_0/ppermute | solution.py:191
  135.1 18.1 %collective-permute-start.22 = (bf16[192,1024]{1,0:T(8,128)(2,1)S(1)}, bf16[192,1024]{1,0:T(8,128)(2,1)S(1)}, u32[]{:S(2)}, u32[]{:S(2)}) collective-permute-start(bf16[192,1024]{1,0:T(8,128)(2,1)S(1)} %pad_maximum_fusion.2.refs_0_), channel_id=1, source_target_pairs={{0,192},{4,68},{8,200},{12,76},{16,208},{20,84},{24,216},{28,92},{... | collective-permute-start | bytes 1179656 | tf_op jit(solution)/shard_map/x_gather_0/ppermute | solution.py:191
  138.4 16.7 %collective-permute-start.21 = (bf16[192,1024]{1,0:T(8,128)(2,1)S(1)}, bf16[192,1024]{1,0:T(8,128)(2,1)}, u32[]{:S(2)}, u32[]{:S(2)}) collective-permute-start(bf16[192,1024]{1,0:T(8,128)(2,1)S(1)} %pad_maximum_fusion.2.refs_0_), channel_id=1, source_target_pairs={{0,128},{4,132},{8,136},{12,140},{16,144},{20,148},{24,152},{28,15... | collective-permute-start | bytes 1179656 | tf_op jit(solution)/shard_map/x_gather_0/ppermute | solution.py:191
  158.7 21.0 %collective-permute-start.29 = (bf16[192,1024]{1,0:T(8,128)(2,1)S(1)}, bf16[192,1024]{1,0:T(8,128)(2,1)S(1)}, u32[]{:S(2)}, u32[]{:S(2)}) collective-permute-start(bf16[192,1024]{1,0:T(8,128)(2,1)S(1)} %pad_maximum_fusion.3.refs_0_), channel_id=1, source_target_pairs={{0,64},{4,196},{8,72},{12,204},{16,80},{20,212},{24,88},{28,220},{... | collective-permute-start | bytes 1179656 | tf_op jit(solution)/shard_map/x_gather_1/ppermute | solution.py:285
  179.7 16.6 %collective-permute-start.31 = (bf16[192,1024]{1,0:T(8,128)(2,1)S(1)}, bf16[192,1024]{1,0:T(8,128)(2,1)S(1)}, u32[]{:S(2)}, u32[]{:S(2)}) collective-permute-start(bf16[192,1024]{1,0:T(8,128)(2,1)S(1)} %pad_maximum_fusion.3.refs_0_), channel_id=1, source_target_pairs={{0,128},{4,132},{8,136},{12,140},{16,144},{20,148},{24,152},{28,15... | collective-permute-start | bytes 1179656 | tf_op jit(solution)/shard_map/x_gather_1/ppermute | solution.py:287
  183.1 13.2 %collective-permute-start.30 = (bf16[192,1024]{1,0:T(8,128)(2,1)S(1)}, bf16[192,1024]{1,0:T(8,128)(2,1)S(1)}, u32[]{:S(2)}, u32[]{:S(2)}) collective-permute-start(bf16[192,1024]{1,0:T(8,128)(2,1)S(1)} %pad_maximum_fusion.3.refs_0_), channel_id=1, source_target_pairs={{0,192},{4,68},{8,200},{12,76},{16,208},{20,84},{24,216},{28,92},{... | collective-permute-start | bytes 1179656 | tf_op jit(solution)/shard_map/x_gather_1/ppermute | solution.py:287
  184.6 12.8 %collective-permute-start.32 = (bf16[192,1024]{1,0:T(8,128)(2,1)S(1)}, bf16[192,1024]{1,0:T(8,128)(2,1)S(1)}, u32[]{:S(2)}, u32[]{:S(2)}) collective-permute-start(bf16[192,1024]{1,0:T(8,128)(2,1)S(1)} %pad_maximum_fusion.3.refs_0_), channel_id=1, source_target_pairs={{0,4},{4,0},{8,12},{12,8},{16,20},{20,16},{24,28},{28,24},{32,36},... | collective-permute-start | bytes 1179656 | tf_op jit(solution)/shard_map/core_gather_1/ppermute | solution.py:195
  (30 other events, 311.0 us)
